TPU v7x, 32 devices: a whole 2x2x4 slice. The times are simulated.
32 devices in a mesh: dp: 2 (over x), row: 4 (over y, core), col: 4 (over z).
Axes of the slice: x: 2, y: 2, z: 4, core: 2. Of those that a mesh axis runs over, the one named last changes fastest.
Arguments:
- grad_parts: float32 [2, 2, 4096, 5120], P('dp', None, 'row', 'col'), may hold values from -6 to 6
- weight: float32 [2, 4096, 5120], P(None, ('row', 'dp'), 'col'), may hold values from -6 to 6
- row_state: float32 [2, 4096], P(None, ('row', 'dp')), may hold values from 0.3 to 8, as said below
- col_state: float32 [2, 5120], P(None, 'col'), may hold values from 0.05 to 0.5
Outputs:
- new_weight: float32 [2, 4096, 5120], P(None, 'row', 'col')
- new_row_state: float32 [2, 4096], P(None, ('row', 'dp'))
- new_col_state: float32 [2, 5120], P(None, 'col')
Inputs may be any that keep to these rules, and one draw needn't show every extreme that they name: `row_state`: positive row moments.
All inputs are finite; a program needn't handle non-finite values.
Results may differ from a plain program's by a relative error of at most 0.00002.
Values sent between devices are 32-bit elements; how exact they have to be, the bound alone decides.
A program may use at most 128 MiB of HBM per device.

v0:
```python
import jax
import jax.numpy as jnp
from jax import lax
from jax.sharding import PartitionSpec as P

D = 4096
FF = 5120


def adafactor(grad, weight, row_state, col_state, reduce_rows, reduce_cols, reduce_all):
    decay = 1.0 - 2.0 ** (-0.8)
    sq = grad * grad + 1e-30
    row_local = jnp.sum(sq, axis=2)
    weight_local = jnp.sum(weight * weight, axis=(1, 2))
    row_total, weight_part = reduce_rows(row_local, weight_local)
    new_row = decay * row_state + (1.0 - decay) * row_total / FF
    col_local = jnp.sum(sq, axis=1)
    moment_local = jnp.sum(new_row, axis=1)
    col_total, moment_total, weight_total = reduce_cols(col_local, moment_local, weight_part)
    new_col = decay * col_state + (1.0 - decay) * col_total / D
    row_mean = moment_total / D
    vhat = new_row[:, :, None] * new_col[:, None, :] / row_mean[:, None, None]
    update = grad / jnp.sqrt(vhat)
    update_total = reduce_all(jnp.sum(update * update, axis=(1, 2)))
    clip = jnp.maximum(1.0, jnp.sqrt(update_total / (D * FF)))
    step_size = 0.3 * jnp.maximum(0.001, jnp.sqrt(weight_total / (D * FF)))
    new_weight = weight - (step_size / clip)[:, None, None] * update
    return (new_weight, new_row, new_col)


def body(grad_parts, weight, row_state, col_state):
    grad = lax.psum_scatter(grad_parts[0], "dp", scatter_dimension=1, tiled=True)

    def reduce_rows(row_local, weight_local):
        return (lax.psum(row_local, "col"), weight_local)

    def reduce_cols(col_local, moment_local, weight_part):
        col_total, moment_total = lax.psum((col_local, moment_local), ("dp", "row"))
        weight_total = lax.psum(weight_part, ("dp", "row", "col"))
        return (col_total, moment_total, weight_total)

    def reduce_all(value):
        return lax.psum(value, ("dp", "row", "col"))

    new_shard, new_row, new_col = adafactor(
        grad, weight, row_state, col_state, reduce_rows, reduce_cols, reduce_all
    )
    new_weight = lax.all_gather(new_shard, "dp", axis=1, tiled=True)
    return (new_weight, new_row, new_col)


def solution(mesh):
    placed = (
        P("dp", None, "row", "col"),
        P(None, ("row", "dp"), "col"),
        P(None, ("row", "dp")),
        P(None, "col"),
    )
    return jax.shard_map(
        body,
        mesh=mesh,
        in_specs=placed,
        out_specs=(P(None, "row", "col"), P(None, ("row", "dp")), P(None, "col")),
        check_vma=False,
    )
```

profile of v0, /device:TPU:0, one launch (start us, length us, event | category | flops | bytes accessed | tf_op | source)
XLA Modules:
  0.0 363.4 jit_solution(12784920032380243132)
XLA Ops:
  7.2 0.0 reduce-scatter.2.cloned.1.call-start
  7.2 0.7 reduce-scatter.2.cloned.1.call-update
  7.9 0.0 copy-start.3
  7.9 0.0 copy-start.2
  7.9 0.0 all-gather.2.cloned.1.call-start
  8.0 3.3 multiply_reduce_fusion.1
  11.2 123.7 %reduce-scatter.2.cloned.1.call-done = f32[2,512,1280]{2,1,0:T(8,128)} async-done(((f32[2,1024,1280]{2,1,0:T(8,128)}), f32[2,512,1280]{2,1,0:T(8,128)}) %reduce-scatter.2.cloned.1.call-update) | async-done | bytes 5242896 | tf_op jit(solution)/shard_map/reduce_scatter | solution.py:32
  134.9 3.4 fusion
  138.3 11.7 %psum.36 = f32[2,512]{1,0:T(2,128)S(1)} all-reduce(f32[2,512]{1,0:T(2,128)S(1)} %get-tuple-element.4), channel_id=1, replica_groups=mesh['dp'=2,'row'=4,'col'=4] {'col'}, use_global_device_ids=true, to_apply=%region_4.0 | all-reduce | flops 1024 | bytes 8192 | tf_op jit(solution)/shard_map/psum | solution.py:35
  150.0 0.0 copy-done.3
  150.0 0.1 fusion.2
  150.1 0.0 copy-start.1
  150.1 22.3 %all-reduce.1 = (f32[2]{0:T(128)S(1)}, f32[2,1280]{1,0:T(2,128)S(1)}) all-reduce(f32[2]{0:T(128)S(1)} %get-tuple-element.9, f32[2,1280]{1,0:T(2,128)S(1)} %get-tuple-element.3), channel_id=1, replica_groups=mesh['dp'=2,'row'=4,'col'=4] {'dp','row'}, use_global_device_ids=true, to_apply=%region_8.0 | all-reduce | flops 2562 | bytes 20496 | tf_op jit(solution)/shard_map/psum | solution.py:38
  172.4 0.0 copy-done.2
  172.4 0.0 copy-start
  172.5 3.9 %multiply_reduce_fusion = f32[2]{0:T(128)S(1)} fusion(f32[2,512,1280]{2,1,0:T(8,128)} %reduce-scatter.2.cloned.1.call-done, f32[2]{0:T(128)S(1)} %broadcast_multiply_fusion, f32[2,1280]{1,0:T(2,128)S(1)} %multiply_add_fusion.1, f32[2,512]{1,0:T(2,128)S(1)} %get-tuple-element.15), kind=kLoop, calls=%fused_computation.1 | loop fusion | flops 6553598 | bytes 5257232 | tf_op jit(solution)/shard_map/reduce_sum | solution.py:24
  176.3 36.8 %all-reduce = (f32[2]{0:T(128)S(1)}, f32[2]{0:T(128)S(1)}) all-reduce(f32[2]{0:T(128)S(1)} %multiply_reduce_fusion, f32[2]{0:T(128)S(1)} %multiply_reduce_fusion.1), channel_id=1, replica_groups=mesh['dp'=2,'row'=4,'col'=4] {'dp','row','col'}, use_global_device_ids=true, to_apply=%region_10.0 | all-reduce | flops 4 | bytes 32 | tf_op jit(solution)/shard_map/psum | solution.py:43
  213.2 6.2 %multiply_subtract_fusion = f32[2,512,1280]{2,1,0:T(8,128)} fusion(f32[2,512,1280]{2,1,0:T(8,128)} %param.5, f32[2]{0:T(128)S(1)} %maximum_divide_fusion, f32[2,512,1280]{2,1,0:T(8,128)} %reduce-scatter.2.cloned.1.call-done, f32[2]{0:T(128)S(1)} %broadcast_multiply_fusion, f32[2,1280]{1,0:T(2,128)S(1)} %multiply_add_fusion.1, f32[2,512]{1,0:T(2,128)S(1)} %get-tuple-element.15), kind=kLoop, calls=%fused_computation | loop fusion | flops 6553600 | bytes 15742992 | tf_op jit(solution)/shard_map/sub | solution.py:27
  219.3 0.0 copy-done.1
  219.3 0.0 copy-done
  219.3 0.0 all-gather.2.cloned.1.call-update
  219.3 128.5 %all-gather.2.cloned.1.call-done = f32[2,1024,1280]{2,1,0:T(8,128)} async-done(((f32[2,512,1280]{2,1,0:T(8,128)}), f32[2,1024,1280]{2,1,0:T(8,128)}) %all-gather.2.cloned.1.call-update) | async-done | bytes 10485776 | tf_op jit(solution)/shard_map/all_gather | solution.py:48
  347.8 8.7 %copy.8 = f32[2,1024,1280]{2,1,0:T(8,128)} copy(f32[2,1024,1280]{2,1,0:T(8,128)} %all-gather.2.cloned.1.call-done) | data formatting | bytes 20971520
  (3 shorter events, 0.0 us)
Async XLA Ops:
  7.2 127.7 %reduce-scatter.2.cloned.1.call-start = ((), (), s32[]{:S(2)}) async-start(), calls=%async_computation.1 | async-start | bytes 15728640 | tf_op jit(solution)/shard_map/reduce_scatter | solution.py:32
  7.9 142.1 %copy-start.3 = (f32[2,512]{1,0:T(2,128)S(1)}, f32[2,512]{1,0:T(2,128)}, u32[]{:S(2)}) copy-start(f32[2,512]{1,0:T(2,128)} %param.6) | copy-start | bytes 12292
  7.9 164.5 %copy-start.2 = (f32[2,1280]{1,0:T(2,128)S(1)}, f32[2,1280]{1,0:T(2,128)}, u32[]{:S(2)}) copy-start(f32[2,1280]{1,0:T(2,128)} %param.7) | copy-start | bytes 30724
  7.9 339.9 %all-gather.2.cloned.1.call-start = ((), (), s32[]{:S(2)}) async-start(), calls=%async_computation.2 | async-start | bytes 15728640 | tf_op jit(solution)/shard_map/all_gather | solution.py:48
  150.1 69.2 %copy-start.1 = (f32[2,512]{1,0:T(2,128)}, f32[2,512]{1,0:T(2,128)S(1)}, u32[]{:S(2)}) copy-start(f32[2,512]{1,0:T(2,128)S(1)} %get-tuple-element.15) | copy-start | bytes 12292
  172.4 46.9 %copy-start = (f32[2,1280]{1,0:T(2,128)}, f32[2,1280]{1,0:T(2,128)S(1)}, u32[]{:S(2)}) copy-start(f32[2,1280]{1,0:T(2,128)S(1)} %multiply_add_fusion.1) | copy-start | bytes 30724
Sparse Core Ops, SparseCore 0:
  10.3 124.5 reduce-scatter.1
  219.5 128.2 all-gather.1
where the time goes:
time: 364 us; the launch traced here: 363 us
  waiting for transfers between devices  253 us (70%)
  blocking collectives  70.8 us (19%)
  other arithmetic  16.8 us (5%)
  between operations  14.1 us (4%)
  local copies, waits for them, and re-layouts  8.76 us (2%)
    all_gather x1, waiting for transfers between devices, body(): new_weight = lax.all_gather(new_shard, 'dp', axis=1, tiled=True)  128 us
    reduce_scatter x1, waiting for transfers between devices, body(): lax.psum_scatter(grad_parts[0], 'dp', scatter_dimension=1, tiled=True)  124 us
    psum x1, blocking collectives, reduce_all(): return lax.psum(value, ('dp', 'row', 'col'))  36.8 us
    psum x1, blocking collectives, reduce_cols(): col_total, moment_total = lax.psum((col_local, moment_local), ('dp', 'row'))  22.3 us
    psum x1, blocking collectives, reduce_rows(): return (lax.psum(row_local, 'col'), weight_local)  11.7 us
    unnamed x9, local copies, waits for them, and re-layouts  8.76 us
  transfers between devices with their start and end apart: 2, of which 2 were waited for; matrix products, arithmetic and copies ran while one was open for 1% of the time, Pallas kernels for 0%

commit v1 on v0

v1 whole, which is shorter than its diff:
```python
import functools

import jax
import jax.numpy as jnp
from jax import lax
from jax.experimental import pallas as pl
from jax.experimental.pallas import tpu as pltpu
from jax.sharding import PartitionSpec as P

DECAY = 1.0 - 2.0 ** (-0.8)
MESH = pl.DeviceIdType.MESH
LANES = 128
CHUNK = 64
FLIGHT = 2


def adafactor(grad, weight, row_state, col_state, reduce_rows, reduce_cols, reduce_all, width, height):
    sq = grad * grad + 1e-30
    row_local = jnp.sum(sq, axis=2)
    weight_local = jnp.sum(weight * weight, axis=(1, 2))
    row_total, weight_part = reduce_rows(row_local, weight_local)
    new_row = DECAY * row_state + (1.0 - DECAY) * row_total / width
    col_local = jnp.sum(sq, axis=1)
    moment_local = jnp.sum(new_row, axis=1)
    col_total, moment_total, weight_total = reduce_cols(col_local, moment_local, weight_part)
    new_col = DECAY * col_state + (1.0 - DECAY) * col_total / height
    row_mean = moment_total / height
    vhat = new_row[:, :, None] * new_col[:, None, :] / row_mean[:, None, None]
    update = grad / jnp.sqrt(vhat)
    update_total = reduce_all(jnp.sum(update * update, axis=(1, 2)))
    clip = jnp.maximum(1.0, jnp.sqrt(update_total / (height * width)))
    step_size = 0.3 * jnp.maximum(0.001, jnp.sqrt(weight_total / (height * width)))
    new_weight = weight - (step_size / clip)[:, None, None] * update
    return (new_weight, new_row, new_col)


def plain_body(n_row, n_col, grad_parts, weight, row_state, col_state):
    grad = lax.psum_scatter(grad_parts[0], "dp", scatter_dimension=1, tiled=True)

    def reduce_rows(row_local, weight_local):
        return (lax.psum(row_local, "col"), weight_local)

    def reduce_cols(col_local, moment_local, weight_part):
        col_total, moment_total = lax.psum((col_local, moment_local), ("dp", "row"))
        weight_total = lax.psum(weight_part, ("dp", "row", "col"))
        return (col_total, moment_total, weight_total)

    def reduce_all(value):
        return lax.psum(value, ("dp", "row", "col"))

    width = grad_parts.shape[3] * n_col
    height = grad_parts.shape[2] * n_row
    new_shard, new_row, new_col = adafactor(
        grad, weight, row_state, col_state, reduce_rows, reduce_cols, reduce_all, width, height
    )
    new_weight = lax.all_gather(new_shard, "dp", axis=1, tiled=True)
    return (new_weight, new_row, new_col)


def kernel(
    n_row, n_col, gp, w, rs, cs, out, nrow, ncol,
    got, own, wv, part, colacc, colscale, alpha, rowbuf, colbuf, abuf, bbuf,
    load_sem, rs_send, rs_recv, ag_send, ag_recv,
    z_send, z_recv, g_send, g_recv,
):
    experts, half, cols = w.shape
    width, height = cols * n_col, 2 * half * n_row
    group = 2 * n_row
    blocks = half // LANES
    lane_blocks = cols // LANES
    per = half // CHUNK
    total = experts * per
    dp, row, col = lax.axis_index("dp"), lax.axis_index("row"), lax.axis_index("col")
    me = dp * n_row + row
    mine = pl.multiple_of(dp * half, CHUNK)
    theirs = pl.multiple_of((1 - dp) * half, CHUNK)
    partner = {"dp": 1 - dp}

    def col_peer(p):
        return {"col": lax.rem(col + p, n_col)}

    def group_peer(p):
        peer = lax.rem(me + p, group)
        return {"dp": lax.div(peer, n_row), "row": lax.rem(peer, n_row)}

    loads = []
    for e in range(experts):
        loads.append((
            pltpu.make_async_copy(gp.at[0, e, pl.ds(mine, half)], own.at[e], load_sem.at[2 * e]),
            pltpu.make_async_copy(w.at[e], wv.at[e], load_sem.at[2 * e + 1]),
        ))
    for pair in loads:
        for load in pair:
            load.start()

    barrier = pltpu.get_barrier_semaphore()
    for p in range(1, group):
        pl.semaphore_signal(barrier, inc=1, device_id=group_peer(p), device_id_type=MESH)
    for p in range(1, n_col):
        pl.semaphore_signal(barrier, inc=1, device_id=col_peer(p), device_id_type=MESH)
    pl.semaphore_wait(barrier, group + n_col - 2)

    def scatter(s):
        e, k = divmod(s, per)
        return pltpu.make_async_remote_copy(
            src_ref=gp.at[0, e, pl.ds(pl.multiple_of(theirs + k * CHUNK, CHUNK), CHUNK)],
            dst_ref=got.at[e, pl.ds(k * CHUNK, CHUNK)],
            send_sem=rs_send.at[s % FLIGHT], recv_sem=rs_recv.at[s],
            device_id=partner, device_id_type=MESH,
        )

    def gather(a):
        e, k = divmod(a, per)
        rows = out.at[e, pl.ds(pl.multiple_of(mine + k * CHUNK, CHUNK), CHUNK)]
        return pltpu.make_async_remote_copy(
            src_ref=rows,
            dst_ref=rows,
            send_sem=ag_send.at[a % FLIGHT], recv_sem=ag_recv.at[a],
            device_id=partner, device_id_type=MESH,
        )

    def exchange(buf, e, slot, count, peer_of, send, recv, which):
        return [
            pltpu.make_async_remote_copy(
                src_ref=buf.at[e, slot], dst_ref=buf.at[e, slot],
                send_sem=send.at[e, which, p - 1], recv_sem=recv.at[e, which, p - 1],
                device_id=peer_of(p), device_id_type=MESH,
            )
            for p in range(1, count)
        ]

    def row_exchange(e):
        return exchange(rowbuf, e, col, n_col, col_peer, z_send, z_recv, 0)

    def col_exchange(e):
        return exchange(colbuf, e, me, group, group_peer, g_send, g_recv, 0)

    def a_exchange(e):
        return exchange(abuf, e, col, n_col, col_peer, z_send, z_recv, 1)

    def b_exchange(e):
        return exchange(bbuf, e, me, group, group_peer, g_send, g_recv, 1)

    def start_all(copies):
        for copy in copies:
            copy.start()

    def wait_all(copies):
        for copy in copies:
            copy.wait()

    def summed(buf, e, count):
        value = buf[e, 0]
        for i in range(1, count):
            value = value + buf[e, i]
        return value

    def add_chunk(s):
        e, k = divmod(s, per)

        def step(i, acc):
            rows = pl.ds(pl.multiple_of(k * CHUNK + i * 8, 8), 8)
            g = own[e, rows, :] + got[e, rows, :]
            own[e, rows, :] = g
            sq = g * g + 1e-30
            lanes = sq[:, :LANES]
            for j in range(1, lane_blocks):
                lanes = lanes + sq[:, j * LANES:(j + 1) * LANES]
            part[e, rows, :] = lanes
            return acc + sq

        first = jnp.zeros((8, cols), jnp.float32) if k == 0 else colacc[e]
        colacc[e] = lax.fori_loop(0, CHUNK // 8, step, first)

    def moments_out(e):
        colbuf[e, me] = jnp.sum(colacc[e], axis=0, keepdims=True)
        for b in range(blocks):
            block = part[e, b * LANES:(b + 1) * LANES, :]
            rowbuf[e, col, b:b + 1, :] = jnp.sum(block.T, axis=0, keepdims=True)
        start_all(row_exchange(e))
        start_all(col_exchange(e))

    def moments_in(e):
        wait_all(row_exchange(e))
        row_total = summed(rowbuf, e, n_col)
        moment = jnp.zeros((1, LANES), jnp.float32)
        for b in range(blocks):
            at = slice(b * LANES, (b + 1) * LANES)
            new_row = DECAY * rs[e:e + 1, at] + (1.0 - DECAY) * row_total[b:b + 1, :] / width
            nrow[e:e + 1, at] = new_row
            moment = moment + new_row
            part[e, at, :] = jnp.broadcast_to(lax.rsqrt(new_row), (LANES, LANES)).T
        wait_all(col_exchange(e))
        new_col = DECAY * cs[e:e + 1, :] + (1.0 - DECAY) * summed(colbuf, e, group) / height
        ncol[e:e + 1, :] = new_col
        colscale[e] = jnp.broadcast_to(lax.rsqrt(new_col), (8, cols))
        bbuf[e, me, 16:24, :] = jnp.broadcast_to(moment * 0.125, (8, LANES))

    def normalise(e):
        loads[e][1].wait()

        def step(i, sums):
            upd, wgt = sums
            rows = pl.ds(pl.multiple_of(i * 8, 8), 8)
            scale = part[e, rows, :]
            for j in range(lane_blocks):
                at = slice(j * LANES, (j + 1) * LANES)
                t = own[e, rows, at] * (scale * colscale[e, :, at])
                own[e, rows, at] = t
                upd = upd + t * t
                v = wv[e, rows, at]
                wgt = wgt + v * v
            return upd, wgt

        zero = jnp.zeros((8, LANES), jnp.float32)
        upd, wgt = lax.fori_loop(0, half // 8, step, (zero, zero))
        abuf[e, col, 0:8, :] = upd
        abuf[e, col, 8:16, :] = wgt
        start_all(a_exchange(e))

    def tile_sums_in(e):
        wait_all(a_exchange(e))
        bbuf[e, me, 0:16, :] = summed(abuf, e, n_col)
        start_all(b_exchange(e))

    def scale_in(e):
        wait_all(b_exchange(e))
        sums = summed(bbuf, e, group)

        def whole(at):
            return jnp.sum(jnp.sum(sums[at:at + 8, :], axis=0, keepdims=True), axis=1, keepdims=True)

        size = float(width * height)
        row_mean = whole(16) / height
        clip = jnp.maximum(1.0, jnp.sqrt(row_mean * whole(0) / size))
        step_size = 0.3 * jnp.maximum(0.001, jnp.sqrt(whole(8) / size))
        alpha[e] = jnp.broadcast_to(step_size / clip * jnp.sqrt(row_mean), (8, LANES))

    def apply(e):
        def step(i, carry):
            rows = pl.ds(pl.multiple_of(i * 8, 8), 8)
            dest = pl.ds(pl.multiple_of(mine + i * 8, 8), 8)
            a = alpha[e]
            for j in range(lane_blocks):
                at = slice(j * LANES, (j + 1) * LANES)
                out[e, dest, at] = wv[e, rows, at] - a * own[e, rows, at]
            return carry

        lax.fori_loop(0, half // 8, step, 0)

    def next_send(n):
        if n >= 2 * total:
            return
        if n >= FLIGHT:
            before = n - FLIGHT
            if before < total:
                scatter(before).wait_send()
            else:
                gather(before - total).wait_send()
        if n < total:
            scatter(n).start()
        else:
            gather(n - total).start()

    for n in range(FLIGHT):
        next_send(n)
    after = {
        per - 1: [moments_out],
        per + 1: [moments_in, normalise],
        per + 2: [tile_sums_in],
        per + 3: [scale_in, apply],
    }
    for n in range(2 * total):
        e, k = divmod(n, per)
        if n < total:
            if k == 0:
                loads[e][0].wait()
            scatter(n).wait_recv()
            next_send(n + FLIGHT)
            add_chunk(n)
        else:
            next_send(n + FLIGHT)
        for done in range(experts):
            for task in after.get(n - done * per, []):
                task(done)
    for n in range(2 * total - FLIGHT, 2 * total):
        gather(n - total).wait_send()
    for a in range(total):
        gather(a).wait_recv()


def fused_body(n_row, n_col, grad_parts, weight, row_state, col_state):
    experts, half, cols = weight.shape
    group = 2 * n_row
    blocks = half // LANES
    total = experts * (half // CHUNK)
    f32 = jnp.float32
    hbm = pl.BlockSpec(memory_space=pltpu.HBM)
    vmem = pl.BlockSpec(memory_space=pltpu.VMEM)
    dma = pltpu.SemaphoreType.DMA
    return pl.pallas_call(
        functools.partial(kernel, n_row, n_col),
        out_shape=(
            jax.ShapeDtypeStruct((experts, 2 * half, cols), f32),
            jax.ShapeDtypeStruct(row_state.shape, f32),
            jax.ShapeDtypeStruct(col_state.shape, f32),
        ),
        in_specs=[hbm, hbm, vmem, vmem],
        out_specs=(vmem, vmem, vmem),
        scratch_shapes=[
            pltpu.VMEM((experts, half, cols), f32),
            pltpu.VMEM((experts, half, cols), f32),
            pltpu.VMEM((experts, half, cols), f32),
            pltpu.VMEM((experts, half, LANES), f32),
            pltpu.VMEM((experts, 8, cols), f32),
            pltpu.VMEM((experts, 8, cols), f32),
            pltpu.VMEM((experts, 8, LANES), f32),
            pltpu.VMEM((experts, n_col, blocks, LANES), f32),
            pltpu.VMEM((experts, group, 1, cols), f32),
            pltpu.VMEM((experts, n_col, 16, LANES), f32),
            pltpu.VMEM((experts, group, 24, LANES), f32),
            dma((2 * experts,)),
            dma((FLIGHT,)),
            dma((total,)),
            dma((FLIGHT,)),
            dma((total,)),
            dma((experts, 2, n_col - 1)),
            dma((experts, 2, n_col - 1)),
            dma((experts, 2, group - 1)),
            dma((experts, 2, group - 1)),
        ],
        compiler_params=pltpu.CompilerParams(
            collective_id=0, has_side_effects=True, vmem_limit_bytes=50 * 1024 * 1024
        ),
        cost_estimate=pl.CostEstimate(
            flops=20 * weight.size, bytes_accessed=20 * weight.size, transcendentals=0
        ),
        name="fused_step",
    )(grad_parts, weight, row_state, col_state)


def solution(mesh):
    placed = (
        P("dp", None, "row", "col"),
        P(None, ("row", "dp"), "col"),
        P(None, ("row", "dp")),
        P(None, "col"),
    )
    body = fused_body if mesh.shape["dp"] == 2 else plain_body
    return jax.shard_map(
        functools.partial(body, mesh.shape["row"], mesh.shape["col"]),
        mesh=mesh,
        in_specs=placed,
        out_specs=(P(None, "row", "col"), P(None, ("row", "dp")), P(None, "col")),
        check_vma=False,
    )
```

time: 364 us -> 252 us (0.69)
  waiting for transfers between devices: 253 us -> 0 us
  Pallas kernels: 0 us -> 240 us
  blocking collectives: 70.8 us -> 0 us
  other arithmetic: 16.8 us -> 0 us
  between operations: 14.1 us -> 0.65 us
    pallas_call x0 -> x1, Pallas kernels: none -> 240 us  [fused_body(): pl.pallas_call(functools.partial(kernel, n_row, n_col), out_shape=(jax.Sh...]
    all_gather x1 -> x0, waiting for transfers between devices: 128 us -> none  [body(): new_weight = lax.all_gather(new_shard, 'dp', axis=1, tiled=True)]
    reduce_scatter x1 -> x0, waiting for transfers between devices: 124 us -> none  [body(): lax.psum_scatter(grad_parts[0], 'dp', scatter_dimension=1, tiled=True)]
    psum x3 -> x0, blocking collectives: 70.8 us -> none  [the longest x1 36.8 us: reduce_all(): return lax.psum(value, ('dp', 'row', 'col'))]
    reduce_sum x4 -> x0, other arithmetic: 10.6 us -> none  [the longest x1 3.87 us: adafactor(): update_total = reduce_all(jnp.sum(update * update, axis=(1, 2)))]
    sub x1 -> x0, other arithmetic: 6.15 us -> none  [adafactor(): new_weight = weight - (step_size / clip)[:, None, None] * update]
    unnamed x9 -> x7, local copies, waits for them, and re-layouts: 8.76 us -> 11.3 us
  transfers between devices with their start and end apart: 2 -> 0, of which waited for: 2 -> 0; matrix products, arithmetic and copies ran while one was open for 1% -> 0% of each run, Pallas kernels for 0% -> 0%
where the time goes in v1:
time: 252 us
  Pallas kernels  240 us (95%)
  local copies, waits for them, and re-layouts  11.3 us (4%)
    pallas_call x1, Pallas kernels, fused_body(): pl.pallas_call(functools.partial(kernel, n_row, n_col), out_shape=(jax.Sh...  240 us
    unnamed x7, local copies, waits for them, and re-layouts  11.3 us

profile of v1, /device:TPU:0, one launch (start us, length us, event | category | flops | bytes accessed | tf_op | source)
XLA Modules:
  0.0 251.9 jit_solution(1831887751289800366)
XLA Ops:
  0.6 0.0 copy-start
  0.6 0.7 copy-done
  1.3 0.0 copy-start.1
  1.3 0.7 copy-done.1
  2.0 239.9 %fused_step.1 = (f32[2,1024,1280]{2,1,0:T(8,128)}, f32[2,512]{1,0:T(2,128)S(1)}, f32[2,1280]{1,0:T(2,128)S(1)}) custom-call(f32[1,2,1024,1280]{3,2,1,0:T(8,128)} %gp.1, f32[2,512,1280]{2,1,0:T(8,128)} %w.1, f32[2,512]{1,0:T(2,128)S(1)} %copy-done.1, f32[2,1280]{1,0:T(2,128)S(1)} %copy-done), custom_call_target="tpu_custom_call" | custom-call | flops 26214400 | bytes 26214400 | tf_op jit(solution)/shard_map/fused_step/pallas_call | solution.py:301
  241.9 8.7 %copy.10 = f32[2,1024,1280]{2,1,0:T(8,128)} copy(f32[2,1024,1280]{2,1,0:T(8,128)} %get-tuple-element.6) | data formatting | bytes 20971520
  250.7 0.6 copy.11
  251.3 0.6 copy.12
Async XLA Ops:
  0.6 0.7 copy-start
  1.3 0.7 copy-start.1

commit v2 on v1

--- a/solution.py
+++ b/solution.py
@@ -10,8 +10,9 @@
 DECAY = 1.0 - 2.0 ** (-0.8)
 MESH = pl.DeviceIdType.MESH
 LANES = 128
-CHUNK = 64
-FLIGHT = 2
+CHUNK = 32
+FLIGHT = 4
+PIECE = 512
 
 
 def adafactor(grad, weight, row_state, col_state, reduce_rows, reduce_cols, reduce_all, width, height):
@@ -58,8 +59,8 @@
 
 
 def kernel(
-    n_row, n_col, gp, w, rs, cs, out, nrow, ncol,
-    got, own, wv, part, colacc, colscale, alpha, rowbuf, colbuf, abuf, bbuf,
+    n_row, n_col, gp, w, rs_in, cs_in, out, nrow, ncol,
+    rs, cs, got, own, wv, part, colacc, colscale, alpha, rowbuf, colbuf, abuf, bbuf,
     load_sem, rs_send, rs_recv, ag_send, ag_recv,
     z_send, z_recv, g_send, g_recv,
 ):
@@ -89,9 +90,12 @@
             pltpu.make_async_copy(gp.at[0, e, pl.ds(mine, half)], own.at[e], load_sem.at[2 * e]),
             pltpu.make_async_copy(w.at[e], wv.at[e], load_sem.at[2 * e + 1]),
         ))
-    for pair in loads:
-        for load in pair:
-            load.start()
+    states = (
+        pltpu.make_async_copy(rs_in, rs, load_sem.at[2 * experts]),
+        pltpu.make_async_copy(cs_in, cs, load_sem.at[2 * experts + 1]),
+    )
+    for load in [load for pair in loads for load in pair] + list(states):
+        load.start()
 
     barrier = pltpu.get_barrier_semaphore()
     for p in range(1, group):
@@ -181,6 +185,9 @@
         start_all(col_exchange(e))
 
     def moments_in(e):
+        if e == 0:
+            for load in states:
+                load.wait()
         wait_all(row_exchange(e))
         row_total = summed(rowbuf, e, n_col)
         moment = jnp.zeros((1, LANES), jnp.float32)
@@ -266,9 +273,9 @@
         next_send(n)
     after = {
         per - 1: [moments_out],
-        per + 1: [moments_in, normalise],
-        per + 2: [tile_sums_in],
-        per + 3: [scale_in, apply],
+        per + 5: [moments_in, normalise],
+        per + 7: [tile_sums_in],
+        per + 11: [scale_in, apply],
     }
     for n in range(2 * total):
         e, k = divmod(n, per)
@@ -289,6 +296,43 @@
         gather(a).wait_recv()
 
 
+def write_out(sources, targets, sems):
+    copies = []
+    for source, target in zip(sources, targets):
+        if source.ndim == 3:
+            step = min(PIECE, source.shape[1])
+            for e in range(source.shape[0]):
+                for r in range(0, source.shape[1], step):
+                    copies.append((source.at[e, pl.ds(r, step)], target.at[e, pl.ds(r, step)]))
+        else:
+            copies.append((source, target))
+    copies = [pltpu.make_async_copy(a, b, sems.at[i]) for i, (a, b) in enumerate(copies)]
+    for copy in copies:
+        copy.start()
+    for copy in copies:
+        copy.wait()
+
+
+def writer(a, b, c, x, y, z, sems):
+    write_out((a, b, c), (x, y, z), sems)
+
+
+def written(results):
+    anywhere = pl.BlockSpec(memory_space=pl.ANY)
+    hbm = pl.BlockSpec(memory_space=pltpu.HBM)
+    big = results[0].shape
+    count = big[0] * (big[1] // min(PIECE, big[1])) + 2
+    return pl.pallas_call(
+        writer,
+        out_shape=tuple(jax.ShapeDtypeStruct(r.shape, r.dtype) for r in results),
+        in_specs=[anywhere] * 3,
+        out_specs=(hbm,) * 3,
+        scratch_shapes=[pltpu.SemaphoreType.DMA((count,))],
+        compiler_params=pltpu.CompilerParams(vmem_limit_bytes=1024 * 1024),
+        name="write_out",
+    )(*results)
+
+
 def fused_body(n_row, n_col, grad_parts, weight, row_state, col_state):
     experts, half, cols = weight.shape
     group = 2 * n_row
@@ -298,16 +342,18 @@
     hbm = pl.BlockSpec(memory_space=pltpu.HBM)
     vmem = pl.BlockSpec(memory_space=pltpu.VMEM)
     dma = pltpu.SemaphoreType.DMA
-    return pl.pallas_call(
+    results = pl.pallas_call(
         functools.partial(kernel, n_row, n_col),
         out_shape=(
-            jax.ShapeDtypeStruct((experts, 2 * half, cols), f32),
-            jax.ShapeDtypeStruct(row_state.shape, f32),
-            jax.ShapeDtypeStruct(col_state.shape, f32),
+            pltpu.VMEM((experts, 2 * half, cols), f32),
+            pltpu.VMEM(row_state.shape, f32),
+            pltpu.VMEM(col_state.shape, f32),
         ),
-        in_specs=[hbm, hbm, vmem, vmem],
+        in_specs=[hbm] * 4,
         out_specs=(vmem, vmem, vmem),
         scratch_shapes=[
+            pltpu.VMEM(row_state.shape, f32),
+            pltpu.VMEM(col_state.shape, f32),
             pltpu.VMEM((experts, half, cols), f32),
             pltpu.VMEM((experts, half, cols), f32),
             pltpu.VMEM((experts, half, cols), f32),
@@ -319,7 +365,7 @@
             pltpu.VMEM((experts, group, 1, cols), f32),
             pltpu.VMEM((experts, n_col, 16, LANES), f32),
             pltpu.VMEM((experts, group, 24, LANES), f32),
-            dma((2 * experts,)),
+            dma((2 * experts + 2,)),
             dma((FLIGHT,)),
             dma((total,)),
             dma((FLIGHT,)),
@@ -330,13 +376,17 @@
             dma((experts, 2, group - 1)),
         ],
         compiler_params=pltpu.CompilerParams(
-            collective_id=0, has_side_effects=True, vmem_limit_bytes=50 * 1024 * 1024
+            collective_id=0, has_side_effects=True, vmem_limit_bytes=30 * 1024 * 1024
         ),
         cost_estimate=pl.CostEstimate(
             flops=20 * weight.size, bytes_accessed=20 * weight.size, transcendentals=0
         ),
         name="fused_step",
-    )(grad_parts, weight, row_state, col_state)
+    )(*[
+        pltpu.with_memory_space_constraint(x, pltpu.HBM)
+        for x in (grad_parts, weight, row_state, col_state)
+    ])
+    return written(results)
 
 
 def solution(mesh):

time: 252 us -> 241 us (0.956)
  local copies, waits for them, and re-layouts: 11.3 us -> 0 us
    unnamed x7 -> x0, local copies, waits for them, and re-layouts: 11.3 us -> none
    pallas_call x1 -> x2, Pallas kernels: 240 us -> 240 us  [the longest x1 236 us: fused_body(): pl.pallas_call(functools.partial(kernel, n_row, n_col), out_shape=(pltpu....]
where the time goes in v2:
time: 241 us
  Pallas kernels  240 us (100%)
    pallas_call x1, Pallas kernels, fused_body(): pl.pallas_call(functools.partial(kernel, n_row, n_col), out_shape=(pltpu....  236 us

profile of v2, /device:TPU:0, one launch (start us, length us, event | category | flops | bytes accessed | tf_op | source)
XLA Modules:
  0.0 241.1 jit_solution(16437546515700688082)
XLA Ops:
  0.6 236.4 %fused_step.1 = (f32[2,1024,1280]{2,1,0:T(8,128)S(1)}, f32[2,512]{1,0:T(2,128)S(1)}, f32[2,1280]{1,0:T(2,128)S(1)}) custom-call(f32[1,2,1024,1280]{3,2,1,0:T(8,128)} %gp.1, f32[2,512,1280]{2,1,0:T(8,128)} %w.1, f32[2,512]{1,0:T(2,128)} %rs_in.1, f32[2,1280]{1,0:T(2,128)} %cs_in.1), custom_call_target="tpu_custom_call" | custom-call | flops 26214400 | bytes 26214400 | tf_op jit(solution)/shard_map/fused_step/pallas_call | solution.py:345
  237.0 4.1 %write_out.1 = (f32[2,1024,1280]{2,1,0:T(8,128)}, f32[2,512]{1,0:T(2,128)}, f32[2,1280]{1,0:T(2,128)}) custom-call(f32[2,1024,1280]{2,1,0:T(8,128)S(1)} %get-tuple-element.6.a, f32[2,512]{1,0:T(2,128)S(1)} %get-tuple-element.7.b, f32[2,1280]{1,0:T(2,128)S(1)} %get-tuple-element.8.c), custom_call_target="tpu_custom_call" | custom-call | tf_op jit(solution)/shard_map/write_out/pallas_call | solution.py:325

commit v3 on v2

--- a/solution.py
+++ b/solution.py
@@ -11,8 +11,8 @@
 MESH = pl.DeviceIdType.MESH
 LANES = 128
 CHUNK = 32
-FLIGHT = 4
-PIECE = 512
+FLIGHT = 6
+PIECE = 128
 
 
 def adafactor(grad, weight, row_state, col_state, reduce_rows, reduce_cols, reduce_all, width, height):
@@ -94,8 +94,7 @@
         pltpu.make_async_copy(rs_in, rs, load_sem.at[2 * experts]),
         pltpu.make_async_copy(cs_in, cs, load_sem.at[2 * experts + 1]),
     )
-    for load in [load for pair in loads for load in pair] + list(states):
-        load.start()
+    loads[0][0].start()
 
     barrier = pltpu.get_barrier_semaphore()
     for p in range(1, group):
@@ -271,11 +270,13 @@
 
     for n in range(FLIGHT):
         next_send(n)
+    for load in list(states) + [load for pair in loads for load in pair][1:]:
+        load.start()
     after = {
         per - 1: [moments_out],
         per + 5: [moments_in, normalise],
-        per + 7: [tile_sums_in],
-        per + 11: [scale_in, apply],
+        per + 6: [tile_sums_in],
+        per + 9: [scale_in, apply],
     }
     for n in range(2 * total):
         e, k = divmod(n, per)

time: 241 us -> 241 us (level)
  no operation moved by 1% of the time
where the time goes in v3:
time: 241 us
  Pallas kernels  241 us (100%)
    pallas_call x1, Pallas kernels, fused_body(): pl.pallas_call(functools.partial(kernel, n_row, n_col), out_shape=(pltpu....  236 us

profile of v3, /device:TPU:0, one launch (start us, length us, event | category | flops | bytes accessed | tf_op | source)
XLA Modules:
  0.0 241.2 jit_solution(13017513612759740909)
XLA Ops:
  0.6 236.4 %fused_step.1 = (f32[2,1024,1280]{2,1,0:T(8,128)S(1)}, f32[2,512]{1,0:T(2,128)S(1)}, f32[2,1280]{1,0:T(2,128)S(1)}) custom-call(f32[1,2,1024,1280]{3,2,1,0:T(8,128)} %gp.1, f32[2,512,1280]{2,1,0:T(8,128)} %w.1, f32[2,512]{1,0:T(2,128)} %rs_in.1, f32[2,1280]{1,0:T(2,128)} %cs_in.1), custom_call_target="tpu_custom_call" | custom-call | flops 26214400 | bytes 26214400 | tf_op jit(solution)/shard_map/fused_step/pallas_call | solution.py:346
  237.1 4.1 %write_out.1 = (f32[2,1024,1280]{2,1,0:T(8,128)}, f32[2,512]{1,0:T(2,128)}, f32[2,1280]{1,0:T(2,128)}) custom-call(f32[2,1024,1280]{2,1,0:T(8,128)S(1)} %get-tuple-element.6.a, f32[2,512]{1,0:T(2,128)S(1)} %get-tuple-element.7.b, f32[2,1280]{1,0:T(2,128)S(1)} %get-tuple-element.8.c), custom_call_target="tpu_custom_call" | custom-call | tf_op jit(solution)/shard_map/write_out/pallas_call | solution.py:326

commit v4 on v3

--- a/solution.py
+++ b/solution.py
@@ -11,7 +11,7 @@
 MESH = pl.DeviceIdType.MESH
 LANES = 128
 CHUNK = 32
-FLIGHT = 6
+FLIGHT = 4
 PIECE = 128
 
 
@@ -60,19 +60,17 @@
 
 def kernel(
     n_row, n_col, gp, w, rs_in, cs_in, out, nrow, ncol,
-    rs, cs, got, own, wv, part, colacc, colscale, alpha, rowbuf, colbuf, abuf, bbuf,
+    rs, cs, got, own, wv, part, colacc, colscale, alpha, rowbuf, colbuf, colpair, abuf, bbuf, bpair,
     load_sem, rs_send, rs_recv, ag_send, ag_recv,
-    z_send, z_recv, g_send, g_recv,
+    z_send, z_recv, y_send, y_recv, x_send, x_recv,
 ):
     experts, half, cols = w.shape
     width, height = cols * n_col, 2 * half * n_row
-    group = 2 * n_row
     blocks = half // LANES
     lane_blocks = cols // LANES
     per = half // CHUNK
     total = experts * per
     dp, row, col = lax.axis_index("dp"), lax.axis_index("row"), lax.axis_index("col")
-    me = dp * n_row + row
     mine = pl.multiple_of(dp * half, CHUNK)
     theirs = pl.multiple_of((1 - dp) * half, CHUNK)
     partner = {"dp": 1 - dp}
@@ -80,9 +78,11 @@
     def col_peer(p):
         return {"col": lax.rem(col + p, n_col)}
 
-    def group_peer(p):
-        peer = lax.rem(me + p, group)
-        return {"dp": lax.div(peer, n_row), "row": lax.rem(peer, n_row)}
+    def row_peer(p):
+        return {"row": lax.rem(row + p, n_row)}
+
+    def dp_peer(p):
+        return partner
 
     loads = []
     for e in range(experts):
@@ -97,11 +97,12 @@
     loads[0][0].start()
 
     barrier = pltpu.get_barrier_semaphore()
-    for p in range(1, group):
-        pl.semaphore_signal(barrier, inc=1, device_id=group_peer(p), device_id_type=MESH)
+    pl.semaphore_signal(barrier, inc=1, device_id=partner, device_id_type=MESH)
     for p in range(1, n_col):
         pl.semaphore_signal(barrier, inc=1, device_id=col_peer(p), device_id_type=MESH)
-    pl.semaphore_wait(barrier, group + n_col - 2)
+    for p in range(1, n_row):
+        pl.semaphore_signal(barrier, inc=1, device_id=row_peer(p), device_id_type=MESH)
+    pl.semaphore_wait(barrier, n_row + n_col - 1)
 
     def scatter(s):
         e, k = divmod(s, per)
@@ -136,13 +137,19 @@
         return exchange(rowbuf, e, col, n_col, col_peer, z_send, z_recv, 0)
 
     def col_exchange(e):
-        return exchange(colbuf, e, me, group, group_peer, g_send, g_recv, 0)
+        return exchange(colbuf, e, row, n_row, row_peer, y_send, y_recv, 0)
+
+    def col_pair(e):
+        return exchange(colpair, e, dp, 2, dp_peer, x_send, x_recv, 0)
 
     def a_exchange(e):
         return exchange(abuf, e, col, n_col, col_peer, z_send, z_recv, 1)
 
     def b_exchange(e):
-        return exchange(bbuf, e, me, group, group_peer, g_send, g_recv, 1)
+        return exchange(bbuf, e, row, n_row, row_peer, y_send, y_recv, 1)
+
+    def b_pair(e):
+        return exchange(bpair, e, dp, 2, dp_peer, x_send, x_recv, 1)
 
     def start_all(copies):
         for copy in copies:
@@ -176,12 +183,17 @@
         colacc[e] = lax.fori_loop(0, CHUNK // 8, step, first)
 
     def moments_out(e):
-        colbuf[e, me] = jnp.sum(colacc[e], axis=0, keepdims=True)
+        colbuf[e, row] = jnp.sum(colacc[e], axis=0, keepdims=True)
         for b in range(blocks):
             block = part[e, b * LANES:(b + 1) * LANES, :]
             rowbuf[e, col, b:b + 1, :] = jnp.sum(block.T, axis=0, keepdims=True)
         start_all(row_exchange(e))
         start_all(col_exchange(e))
+
+    def columns_in(e):
+        wait_all(col_exchange(e))
+        colpair[e, dp] = summed(colbuf, e, n_row)
+        start_all(col_pair(e))
 
     def moments_in(e):
         if e == 0:
@@ -196,11 +208,11 @@
             nrow[e:e + 1, at] = new_row
             moment = moment + new_row
             part[e, at, :] = jnp.broadcast_to(lax.rsqrt(new_row), (LANES, LANES)).T
-        wait_all(col_exchange(e))
-        new_col = DECAY * cs[e:e + 1, :] + (1.0 - DECAY) * summed(colbuf, e, group) / height
+        wait_all(col_pair(e))
+        new_col = DECAY * cs[e:e + 1, :] + (1.0 - DECAY) * summed(colpair, e, 2) / height
         ncol[e:e + 1, :] = new_col
         colscale[e] = jnp.broadcast_to(lax.rsqrt(new_col), (8, cols))
-        bbuf[e, me, 16:24, :] = jnp.broadcast_to(moment * 0.125, (8, LANES))
+        bbuf[e, row, 2:3, :] = moment
 
     def normalise(e):
         loads[e][1].wait()
@@ -220,26 +232,31 @@
 
         zero = jnp.zeros((8, LANES), jnp.float32)
         upd, wgt = lax.fori_loop(0, half // 8, step, (zero, zero))
-        abuf[e, col, 0:8, :] = upd
-        abuf[e, col, 8:16, :] = wgt
+        abuf[e, col, 0:1, :] = jnp.sum(upd, axis=0, keepdims=True)
+        abuf[e, col, 1:2, :] = jnp.sum(wgt, axis=0, keepdims=True)
         start_all(a_exchange(e))
 
     def tile_sums_in(e):
         wait_all(a_exchange(e))
-        bbuf[e, me, 0:16, :] = summed(abuf, e, n_col)
+        bbuf[e, row, 0:2, :] = summed(abuf, e, n_col)
         start_all(b_exchange(e))
 
+    def plane_sums_in(e):
+        wait_all(b_exchange(e))
+        bpair[e, dp] = summed(bbuf, e, n_row)
+        start_all(b_pair(e))
+
     def scale_in(e):
-        wait_all(b_exchange(e))
-        sums = summed(bbuf, e, group)
+        wait_all(b_pair(e))
+        sums = jnp.sum(summed(bpair, e, 2), axis=1, keepdims=True)
 
         def whole(at):
-            return jnp.sum(jnp.sum(sums[at:at + 8, :], axis=0, keepdims=True), axis=1, keepdims=True)
+            return sums[at:at + 1, :]
 
         size = float(width * height)
-        row_mean = whole(16) / height
+        row_mean = whole(2) / height
         clip = jnp.maximum(1.0, jnp.sqrt(row_mean * whole(0) / size))
-        step_size = 0.3 * jnp.maximum(0.001, jnp.sqrt(whole(8) / size))
+        step_size = 0.3 * jnp.maximum(0.001, jnp.sqrt(whole(1) / size))
         alpha[e] = jnp.broadcast_to(step_size / clip * jnp.sqrt(row_mean), (8, LANES))
 
     def apply(e):
@@ -274,9 +291,11 @@
         load.start()
     after = {
         per - 1: [moments_out],
+        per + 1: [columns_in],
         per + 5: [moments_in, normalise],
         per + 6: [tile_sums_in],
-        per + 9: [scale_in, apply],
+        per + 7: [plane_sums_in],
+        per + 11: [scale_in, apply],
     }
     for n in range(2 * total):
         e, k = divmod(n, per)
@@ -336,7 +355,6 @@
 
 def fused_body(n_row, n_col, grad_parts, weight, row_state, col_state):
     experts, half, cols = weight.shape
-    group = 2 * n_row
     blocks = half // LANES
     total = experts * (half // CHUNK)
     f32 = jnp.float32
@@ -363,9 +381,11 @@
             pltpu.VMEM((experts, 8, cols), f32),
             pltpu.VMEM((experts, 8, LANES), f32),
             pltpu.VMEM((experts, n_col, blocks, LANES), f32),
-            pltpu.VMEM((experts, group, 1, cols), f32),
-            pltpu.VMEM((experts, n_col, 16, LANES), f32),
-            pltpu.VMEM((experts, group, 24, LANES), f32),
+            pltpu.VMEM((experts, n_row, 1, cols), f32),
+            pltpu.VMEM((experts, 2, 1, cols), f32),
+            pltpu.VMEM((experts, n_col, 2, LANES), f32),
+            pltpu.VMEM((experts, n_row, 3, LANES), f32),
+            pltpu.VMEM((experts, 2, 3, LANES), f32),
             dma((2 * experts + 2,)),
             dma((FLIGHT,)),
             dma((total,)),
@@ -373,8 +393,10 @@
             dma((total,)),
             dma((experts, 2, n_col - 1)),
             dma((experts, 2, n_col - 1)),
-            dma((experts, 2, group - 1)),
-            dma((experts, 2, group - 1)),
+            dma((experts, 2, n_row - 1)),
+            dma((experts, 2, n_row - 1)),
+            dma((experts, 2, 1)),
+            dma((experts, 2, 1)),
         ],
         compiler_params=pltpu.CompilerParams(
             collective_id=0, has_side_effects=True, vmem_limit_bytes=30 * 1024 * 1024

time: 241 us -> 238 us (0.988)
  Pallas kernels: 241 us -> 237 us
    pallas_call x1, Pallas kernels: 236 us -> 233 us  [fused_body(): pl.pallas_call(functools.partial(kernel, n_row, n_col), out_shape=(pltpu....]
where the time goes in v4:
time: 238 us
  Pallas kernels  237 us (100%)
    pallas_call x1, Pallas kernels, fused_body(): pl.pallas_call(functools.partial(kernel, n_row, n_col), out_shape=(pltpu....  233 us

profile of v4, /device:TPU:0, one launch (start us, length us, event | category | flops | bytes accessed | tf_op | source)
XLA Modules:
  0.0 238.1 jit_solution(14149879798660695938)
XLA Ops:
  0.6 233.4 %fused_step.1 = (f32[2,1024,1280]{2,1,0:T(8,128)S(1)}, f32[2,512]{1,0:T(2,128)S(1)}, f32[2,1280]{1,0:T(2,128)S(1)}) custom-call(f32[1,2,1024,1280]{3,2,1,0:T(8,128)} %gp.1, f32[2,512,1280]{2,1,0:T(8,128)} %w.1, f32[2,512]{1,0:T(2,128)} %rs_in.1, f32[2,1280]{1,0:T(2,128)} %cs_in.1), custom_call_target="tpu_custom_call" | custom-call | flops 26214400 | bytes 26214400 | tf_op jit(solution)/shard_map/fused_step/pallas_call | solution.py:364
  234.0 4.1 %write_out.1 = (f32[2,1024,1280]{2,1,0:T(8,128)}, f32[2,512]{1,0:T(2,128)}, f32[2,1280]{1,0:T(2,128)}) custom-call(f32[2,1024,1280]{2,1,0:T(8,128)S(1)} %get-tuple-element.6.a, f32[2,512]{1,0:T(2,128)S(1)} %get-tuple-element.7.b, f32[2,1280]{1,0:T(2,128)S(1)} %get-tuple-element.8.c), custom_call_target="tpu_custom_call" | custom-call | tf_op jit(solution)/shard_map/write_out/pallas_call | solution.py:345

commit v5 on v4

--- a/solution.py
+++ b/solution.py
@@ -13,6 +13,7 @@
 CHUNK = 32
 FLIGHT = 4
 PIECE = 128
+TAIL = 4
 
 
 def adafactor(grad, weight, row_state, col_state, reduce_rows, reduce_cols, reduce_all, width, height):
@@ -59,9 +60,9 @@
 
 
 def kernel(
-    n_row, n_col, gp, w, rs_in, cs_in, out, nrow, ncol,
+    n_row, n_col, gp, w, rs_in, cs_in, out, nrow, ncol, tail,
     rs, cs, got, own, wv, part, colacc, colscale, alpha, rowbuf, colbuf, colpair, abuf, bbuf, bpair,
-    load_sem, rs_send, rs_recv, ag_send, ag_recv,
+    load_sem, tail_sem, rs_send, rs_recv, ag_send, ag_recv,
     z_send, z_recv, y_send, y_recv, x_send, x_recv,
 ):
     experts, half, cols = w.shape
@@ -270,9 +271,15 @@
             return carry
 
         lax.fori_loop(0, half // 8, step, 0)
+        if e == experts - 1:
+            tail_copy().start()
+
+    def tail_copy():
+        rows = pl.ds(pl.multiple_of(mine + half - TAIL * CHUNK, CHUNK), TAIL * CHUNK)
+        return pltpu.make_async_copy(out.at[experts - 1, rows], tail, tail_sem)
 
     def next_send(n):
-        if n >= 2 * total:
+        if n >= 2 * total - TAIL:
             return
         if n >= FLIGHT:
             before = n - FLIGHT
@@ -310,9 +317,10 @@
         for done in range(experts):
             for task in after.get(n - done * per, []):
                 task(done)
-    for n in range(2 * total - FLIGHT, 2 * total):
+    tail_copy().wait()
+    for n in range(2 * total - TAIL - FLIGHT, 2 * total - TAIL):
         gather(n - total).wait_send()
-    for a in range(total):
+    for a in range(total - TAIL):
         gather(a).wait_recv()
 
 
@@ -349,6 +357,9 @@
         out_specs=(hbm,) * 3,
         scratch_shapes=[pltpu.SemaphoreType.DMA((count,))],
         compiler_params=pltpu.CompilerParams(vmem_limit_bytes=1024 * 1024),
+        cost_estimate=pl.CostEstimate(
+            flops=0, bytes_accessed=8 * results[0].size, transcendentals=0
+        ),
         name="write_out",
     )(*results)
 
@@ -367,9 +378,10 @@
             pltpu.VMEM((experts, 2 * half, cols), f32),
             pltpu.VMEM(row_state.shape, f32),
             pltpu.VMEM(col_state.shape, f32),
+            pltpu.HBM((TAIL * CHUNK, cols), f32),
         ),
         in_specs=[hbm] * 4,
-        out_specs=(vmem, vmem, vmem),
+        out_specs=(vmem, vmem, vmem, hbm),
         scratch_shapes=[
             pltpu.VMEM(row_state.shape, f32),
             pltpu.VMEM(col_state.shape, f32),
@@ -387,6 +399,7 @@
             pltpu.VMEM((experts, n_row, 3, LANES), f32),
             pltpu.VMEM((experts, 2, 3, LANES), f32),
             dma((2 * experts + 2,)),
+            dma,
             dma((FLIGHT,)),
             dma((total,)),
             dma((FLIGHT,)),
@@ -409,7 +422,11 @@
         pltpu.with_memory_space_constraint(x, pltpu.HBM)
         for x in (grad_parts, weight, row_state, col_state)
     ])
-    return written(results)
+    arriving = lax.ppermute(results[3], "dp", [(0, 1), (1, 0)])
+    new_weight, new_row, new_col = written(results[:3])
+    start = (1 - lax.axis_index("dp")) * half + half - TAIL * CHUNK
+    new_weight = lax.dynamic_update_slice(new_weight, arriving[None], (experts - 1, start, 0))
+    return (new_weight, new_row, new_col)
 
 
 def solution(mesh):

time: 238 us -> 241 us (1.013)
  Pallas kernels: 237 us -> 223 us
  local copies, waits for them, and re-layouts: 0 us -> 8.94 us
  waiting for transfers between devices: 0 us -> 7.21 us
    pallas_call x1, Pallas kernels: 233 us -> 219 us  [fused_body(): pl.pallas_call(functools.partial(kernel, n_row, n_col), out_shape=(pltpu....]
    unnamed x0 -> x4, local copies, waits for them, and re-layouts: none -> 8.06 us
    ppermute x0 -> x1, waiting for transfers between devices: none -> 7.21 us  [fused_body(): arriving = lax.ppermute(results[3], 'dp', [(0, 1), (1, 0)])]
  transfers between devices with their start and end apart: 0 -> 1, of which waited for: 0 -> 1; matrix products, arithmetic and copies ran while one was open for 0% -> 0% of each run, Pallas kernels for 0% -> 2%
where the time goes in v5:
time: 241 us
  Pallas kernels  223 us (93%)
  local copies, waits for them, and re-layouts  8.94 us (4%)
  waiting for transfers between devices  7.21 us (3%)
    pallas_call x1, Pallas kernels, fused_body(): pl.pallas_call(functools.partial(kernel, n_row, n_col), out_shape=(pltpu....  219 us
    unnamed x4, local copies, waits for them, and re-layouts  8.06 us
    ppermute x1, waiting for transfers between devices, fused_body(): arriving = lax.ppermute(results[3], 'dp', [(0, 1), (1, 0)])  7.21 us
  transfers between devices with their start and end apart: 1, of which 1 were waited for; matrix products, arithmetic and copies ran while one was open for 0% of the time, Pallas kernels for 2%

profile of v5, /device:TPU:0, one launch (start us, length us, event | category | flops | bytes accessed | tf_op | source)
XLA Modules:
  0.0 240.8 jit_solution(17758475228682341812)
XLA Ops:
  0.6 219.4 %fused_step.1 = (f32[2,1024,1280]{2,1,0:T(8,128)S(1)}, f32[2,512]{1,0:T(2,128)S(1)}, f32[2,1280]{1,0:T(2,128)S(1)}, f32[128,1280]{1,0:T(8,128)}) custom-call(f32[1,2,1024,1280]{3,2,1,0:T(8,128)} %gp.1, f32[2,512,1280]{2,1,0:T(8,128)} %w.1, f32[2,512]{1,0:T(2,128)} %rs_in.1, f32[2,1280]{1,0:T(2,128)} %cs_in.1), custom_call_target="tpu_custom_call" | custom-call | flops 26214400 | bytes 26214400 | tf_op jit(solution)/shard_map/fused_step/pallas_call | solution.py:375
  220.0 0.0 copy-start
  220.0 4.1 %copy-done = f32[2,1024,1280]{2,1,0:T(8,128)} copy-done((f32[2,1024,1280]{2,1,0:T(8,128)}, f32[2,1024,1280]{2,1,0:T(8,128)S(1)}, u32[]{:S(2)}) %copy-start) | copy-done | bytes 10485784
  224.1 0.5 collective-permute-start
  224.6 0.0 copy-start.1
  224.6 4.0 %copy-done.1 = f32[2,1024,1280]{2,1,0:T(8,128)S(1)} copy-done((f32[2,1024,1280]{2,1,0:T(8,128)S(1)}, f32[2,1024,1280]{2,1,0:T(8,128)}, u32[]{:S(2)}) %copy-start.1) | copy-done | bytes 10485784
  228.6 4.1 %write_out.1 = (f32[2,1024,1280]{2,1,0:T(8,128)}, f32[2,512]{1,0:T(2,128)}, f32[2,1280]{1,0:T(2,128)}) custom-call(f32[2,1024,1280]{2,1,0:T(8,128)S(1)} %copy-done.1, f32[2,512]{1,0:T(2,128)S(1)} %get-tuple-element.11.b, f32[2,1280]{1,0:T(2,128)S(1)} %get-tuple-element.12.c), custom_call_target="tpu_custom_call" | custom-call | bytes 20971520 | tf_op jit(solution)/shard_map/write_out/pallas_call | solution.py:353
  232.7 7.2 %collective-permute-done = f32[128,1280]{1,0:T(8,128)S(1)} collective-permute-done((f32[128,1280]{1,0:T(8,128)}, f32[128,1280]{1,0:T(8,128)S(1)}, u32[]{:S(2)}, u32[]{:S(2)}) %collective-permute-start) | collective-permute-done | bytes 655392 | tf_op jit(solution)/shard_map/ppermute | solution.py:425
  239.9 0.9 bitcast_dynamic-update-slice_fusion
Async XLA Ops:
  220.0 4.1 %copy-start = (f32[2,1024,1280]{2,1,0:T(8,128)}, f32[2,1024,1280]{2,1,0:T(8,128)S(1)}, u32[]{:S(2)}) copy-start(f32[2,1024,1280]{2,1,0:T(8,128)S(1)} %get-tuple-element.10.a) | copy-start | bytes 31457284
  224.1 15.8 %collective-permute-start = (f32[128,1280]{1,0:T(8,128)}, f32[128,1280]{1,0:T(8,128)S(1)}, u32[]{:S(2)}, u32[]{:S(2)}) collective-permute-start(f32[128,1280]{1,0:T(8,128)} %get-tuple-element.14), channel_id=1, source_target_pairs={{0,16},{16,0},{1,17},{17,1},{2,18},{18,2},{3,19},{19,3},{4,20},{20... | collective-permute-start | bytes 1966088 | tf_op jit(solution)/shard_map/ppermute | solution.py:425
  224.6 4.0 %copy-start.1 = (f32[2,1024,1280]{2,1,0:T(8,128)S(1)}, f32[2,1024,1280]{2,1,0:T(8,128)}, u32[]{:S(2)}) copy-start(f32[2,1024,1280]{2,1,0:T(8,128)} %copy-done) | copy-start | bytes 31457284

commit v6 on v5

--- a/solution.py
+++ b/solution.py
@@ -62,7 +62,7 @@
 def kernel(
     n_row, n_col, gp, w, rs_in, cs_in, out, nrow, ncol, tail,
     rs, cs, got, own, wv, part, colacc, colscale, alpha, rowbuf, colbuf, colpair, abuf, bbuf, bpair,
-    load_sem, tail_sem, rs_send, rs_recv, ag_send, ag_recv,
+    load_sem, store_sem, tail_sem, rs_send, rs_recv, ag_send, ag_recv,
     z_send, z_recv, y_send, y_recv, x_send, x_recv,
 ):
     experts, half, cols = w.shape
@@ -116,10 +116,9 @@
 
     def gather(a):
         e, k = divmod(a, per)
-        rows = out.at[e, pl.ds(pl.multiple_of(mine + k * CHUNK, CHUNK), CHUNK)]
         return pltpu.make_async_remote_copy(
-            src_ref=rows,
-            dst_ref=rows,
+            src_ref=wv.at[e, pl.ds(k * CHUNK, CHUNK)],
+            dst_ref=out.at[e, pl.ds(pl.multiple_of(mine + k * CHUNK, CHUNK), CHUNK)],
             send_sem=ag_send.at[a % FLIGHT], recv_sem=ag_recv.at[a],
             device_id=partner, device_id_type=MESH,
         )
@@ -263,20 +262,23 @@
     def apply(e):
         def step(i, carry):
             rows = pl.ds(pl.multiple_of(i * 8, 8), 8)
-            dest = pl.ds(pl.multiple_of(mine + i * 8, 8), 8)
             a = alpha[e]
             for j in range(lane_blocks):
                 at = slice(j * LANES, (j + 1) * LANES)
-                out[e, dest, at] = wv[e, rows, at] - a * own[e, rows, at]
+                wv[e, rows, at] = wv[e, rows, at] - a * own[e, rows, at]
             return carry
 
         lax.fori_loop(0, half // 8, step, 0)
         if e == experts - 1:
             tail_copy().start()
+        keep(e).start()
 
     def tail_copy():
-        rows = pl.ds(pl.multiple_of(mine + half - TAIL * CHUNK, CHUNK), TAIL * CHUNK)
-        return pltpu.make_async_copy(out.at[experts - 1, rows], tail, tail_sem)
+        rows = pl.ds(half - TAIL * CHUNK, TAIL * CHUNK)
+        return pltpu.make_async_copy(wv.at[experts - 1, rows], tail, tail_sem)
+
+    def keep(e):
+        return pltpu.make_async_copy(wv.at[e], out.at[e, pl.ds(mine, half)], store_sem.at[e])
 
     def next_send(n):
         if n >= 2 * total - TAIL:
@@ -318,6 +320,8 @@
             for task in after.get(n - done * per, []):
                 task(done)
     tail_copy().wait()
+    for e in range(experts):
+        keep(e).wait()
     for n in range(2 * total - TAIL - FLIGHT, 2 * total - TAIL):
         gather(n - total).wait_send()
     for a in range(total - TAIL):
@@ -361,7 +365,7 @@
             flops=0, bytes_accessed=8 * results[0].size, transcendentals=0
         ),
         name="write_out",
-    )(*results)
+    )(pltpu.with_memory_space_constraint(results[0], pltpu.HBM), *results[1:])
 
 
 def fused_body(n_row, n_col, grad_parts, weight, row_state, col_state):
@@ -375,13 +379,13 @@
     results = pl.pallas_call(
         functools.partial(kernel, n_row, n_col),
         out_shape=(
-            pltpu.VMEM((experts, 2 * half, cols), f32),
+            pltpu.HBM((experts, 2 * half, cols), f32),
             pltpu.VMEM(row_state.shape, f32),
             pltpu.VMEM(col_state.shape, f32),
             pltpu.HBM((TAIL * CHUNK, cols), f32),
         ),
         in_specs=[hbm] * 4,
-        out_specs=(vmem, vmem, vmem, hbm),
+        out_specs=(hbm, vmem, vmem, hbm),
         scratch_shapes=[
             pltpu.VMEM(row_state.shape, f32),
             pltpu.VMEM(col_state.shape, f32),
@@ -399,6 +403,7 @@
             pltpu.VMEM((experts, n_row, 3, LANES), f32),
             pltpu.VMEM((experts, 2, 3, LANES), f32),
             dma((2 * experts + 2,)),
+            dma((experts,)),
             dma,
             dma((FLIGHT,)),
             dma((total,)),

time: 241 us -> 541 us (2.24)
  Pallas kernels: 223 us -> 538 us
  local copies, waits for them, and re-layouts: 8.94 us -> 0.89 us
  waiting for transfers between devices: 7.21 us -> 0.01 us
    pallas_call x1, Pallas kernels: 4.08 us -> 319 us  [written(): pl.pallas_call(writer, out_shape=tuple((jax.ShapeDtypeStruct(r.shape, r.d...]
    unnamed x4 -> x0, local copies, waits for them, and re-layouts: 8.06 us -> none
    ppermute x1, waiting for transfers between devices: 7.21 us -> 0.01 us  [fused_body(): arriving = lax.ppermute(results[3], 'dp', [(0, 1), (1, 0)])]
  transfers between devices with their start and end apart: 1 -> 1, of which waited for: 1 -> 0; matrix products, arithmetic and copies ran while one was open for 0% -> 0% of each run, Pallas kernels for 2% -> 59%
where the time goes in v6:
time: 541 us
  Pallas kernels  538 us (99%)
    pallas_call x1, Pallas kernels, written(): pl.pallas_call(writer, out_shape=tuple((jax.ShapeDtypeStruct(r.shape, r.d...  319 us
    pallas_call x1, Pallas kernels, fused_body(): pl.pallas_call(functools.partial(kernel, n_row, n_col), out_shape=(pltpu....  219 us
  transfers between devices with their start and end apart: 1, of which 0 were waited for; matrix products, arithmetic and copies ran while one was open for 0% of the time, Pallas kernels for 59%

profile of v6, /device:TPU:0, one launch (start us, length us, event | category | flops | bytes accessed | tf_op | source)
XLA Modules:
  0.0 540.5 jit_solution(5787653829970443325)
XLA Ops:
  0.6 219.5 %fused_step.1 = (f32[2,1024,1280]{2,1,0:T(8,128)}, f32[2,512]{1,0:T(2,128)S(1)}, f32[2,1280]{1,0:T(2,128)S(1)}, f32[128,1280]{1,0:T(8,128)}) custom-call(f32[1,2,1024,1280]{3,2,1,0:T(8,128)} %gp.1, f32[2,512,1280]{2,1,0:T(8,128)} %w.1, f32[2,512]{1,0:T(2,128)} %rs_in.1, f32[2,1280]{1,0:T(2,128)} %cs_in.1), custom_call_target="tpu_custom_call" | custom-call | flops 26214400 | bytes 26214400 | tf_op jit(solution)/shard_map/fused_step/pallas_call | solution.py:379
  220.1 0.6 collective-permute-start
  220.7 318.9 %write_out.1 = (f32[2,1024,1280]{2,1,0:T(8,128)}, f32[2,512]{1,0:T(2,128)}, f32[2,1280]{1,0:T(2,128)}) custom-call(f32[2,1024,1280]{2,1,0:T(8,128)} %get-tuple-element.10.a, f32[2,512]{1,0:T(2,128)S(1)} %get-tuple-element.11.b, f32[2,1280]{1,0:T(2,128)S(1)} %get-tuple-element.12.c), custom_call_target="tpu_custom_call" | custom-call | bytes 20971520 | tf_op jit(solution)/shard_map/write_out/pallas_call | solution.py:357
  539.6 0.0 collective-permute-done
  539.6 0.9 bitcast_dynamic-update-slice_fusion
Async XLA Ops:
  220.1 319.5 %collective-permute-start = (f32[128,1280]{1,0:T(8,128)}, f32[128,1280]{1,0:T(8,128)S(1)}, u32[]{:S(2)}, u32[]{:S(2)}) collective-permute-start(f32[128,1280]{1,0:T(8,128)} %get-tuple-element.14), channel_id=1, source_target_pairs={{0,16},{16,0},{1,17},{17,1},{2,18},{18,2},{3,19},{19,3},{4,20},{20... | collective-permute-start | bytes 1966088 | tf_op jit(solution)/shard_map/ppermute | solution.py:430

commit v7 on v6

--- a/solution.py
+++ b/solution.py
@@ -328,44 +328,29 @@
         gather(a).wait_recv()
 
 
-def write_out(sources, targets, sems):
-    copies = []
-    for source, target in zip(sources, targets):
-        if source.ndim == 3:
-            step = min(PIECE, source.shape[1])
-            for e in range(source.shape[0]):
-                for r in range(0, source.shape[1], step):
-                    copies.append((source.at[e, pl.ds(r, step)], target.at[e, pl.ds(r, step)]))
-        else:
-            copies.append((source, target))
-    copies = [pltpu.make_async_copy(a, b, sems.at[i]) for i, (a, b) in enumerate(copies)]
-    for copy in copies:
-        copy.start()
-    for copy in copies:
-        copy.wait()
-
-
-def writer(a, b, c, x, y, z, sems):
-    write_out((a, b, c), (x, y, z), sems)
+def writer(a, b, c, x, y, z):
+    x[...] = a[...]
+    y[...] = b[...]
+    z[...] = c[...]
 
 
 def written(results):
-    anywhere = pl.BlockSpec(memory_space=pl.ANY)
-    hbm = pl.BlockSpec(memory_space=pltpu.HBM)
-    big = results[0].shape
-    count = big[0] * (big[1] // min(PIECE, big[1])) + 2
+    big, row, col = results
+    experts, rows, cols = big.shape
+    tile = pl.BlockSpec((1, PIECE, cols), lambda e, i: (e, i, 0))
+    small = [pl.BlockSpec(r.shape, lambda e, i: (0, 0)) for r in (row, col)]
     return pl.pallas_call(
         writer,
+        grid=(experts, rows // PIECE),
         out_shape=tuple(jax.ShapeDtypeStruct(r.shape, r.dtype) for r in results),
-        in_specs=[anywhere] * 3,
-        out_specs=(hbm,) * 3,
-        scratch_shapes=[pltpu.SemaphoreType.DMA((count,))],
-        compiler_params=pltpu.CompilerParams(vmem_limit_bytes=1024 * 1024),
+        in_specs=[tile] + small,
+        out_specs=(tile, *small),
+        compiler_params=pltpu.CompilerParams(vmem_limit_bytes=8 * 1024 * 1024),
         cost_estimate=pl.CostEstimate(
-            flops=0, bytes_accessed=8 * results[0].size, transcendentals=0
+            flops=0, bytes_accessed=8 * big.size, transcendentals=0
         ),
         name="write_out",
-    )(pltpu.with_memory_space_constraint(results[0], pltpu.HBM), *results[1:])
+    )(pltpu.with_memory_space_constraint(big, pltpu.HBM), row, col)
 
 
 def fused_body(n_row, n_col, grad_parts, weight, row_state, col_state):

time: 541 us -> 237 us (0.44)
  Pallas kernels: 538 us -> 233 us
    pallas_call x1, Pallas kernels: 319 us -> 13.1 us  [written(): pl.pallas_call(writer, grid=(experts, rows // PIECE), out_shape=tuple((ja...]
  transfers between devices with their start and end apart: 1 -> 1, of which waited for: 0 -> 1; matrix products, arithmetic and copies ran while one was open for 0% -> 0% of each run, Pallas kernels for 59% -> 6%
where the time goes in v7:
time: 237 us
  Pallas kernels  233 us (98%)
    pallas_call x1, Pallas kernels, fused_body(): pl.pallas_call(functools.partial(kernel, n_row, n_col), out_shape=(pltpu....  219 us
    pallas_call x1, Pallas kernels, written(): pl.pallas_call(writer, grid=(experts, rows // PIECE), out_shape=tuple((ja...  13.1 us
  transfers between devices with their start and end apart: 1, of which 1 were waited for; matrix products, arithmetic and copies ran while one was open for 0% of the time, Pallas kernels for 6%

profile of v7, /device:TPU:0, one launch (start us, length us, event | category | flops | bytes accessed | tf_op | source)
XLA Modules:
  0.0 236.9 jit_solution(4768433924383648569)
XLA Ops:
  0.6 219.5 %fused_step.1 = (f32[2,1024,1280]{2,1,0:T(8,128)}, f32[2,512]{1,0:T(2,128)S(1)}, f32[2,1280]{1,0:T(2,128)S(1)}, f32[128,1280]{1,0:T(8,128)}) custom-call(f32[1,2,1024,1280]{3,2,1,0:T(8,128)} %gp.1, f32[2,512,1280]{2,1,0:T(8,128)} %w.1, f32[2,512]{1,0:T(2,128)} %rs_in.1, f32[2,1280]{1,0:T(2,128)} %cs_in.1), custom_call_target="tpu_custom_call" | custom-call | flops 26214400 | bytes 26214400 | tf_op jit(solution)/shard_map/fused_step/pallas_call | solution.py:364
  220.1 0.6 collective-permute-start
  220.7 13.1 %write_out.1 = (f32[2,1024,1280]{2,1,0:T(8,128)}, f32[2,512]{1,0:T(2,128)}, f32[2,1280]{1,0:T(2,128)}) custom-call(f32[2,1024,1280]{2,1,0:T(8,128)} %get-tuple-element.10.a, f32[2,512]{1,0:T(2,128)S(1)} %get-tuple-element.11.b, f32[2,1280]{1,0:T(2,128)S(1)} %get-tuple-element.12.c), custom_call_target="tpu_custom_call" | custom-call | bytes 20971520 | tf_op jit(solution)/shard_map/write_out/pallas_call | solution.py:342
  233.8 2.2 collective-permute-done
  236.0 0.9 bitcast_dynamic-update-slice_fusion
Async XLA Ops:
  220.1 15.9 %collective-permute-start = (f32[128,1280]{1,0:T(8,128)}, f32[128,1280]{1,0:T(8,128)S(1)}, u32[]{:S(2)}, u32[]{:S(2)}) collective-permute-start(f32[128,1280]{1,0:T(8,128)} %get-tuple-element.14), channel_id=1, source_target_pairs={{0,16},{16,0},{1,17},{17,1},{2,18},{18,2},{3,19},{19,3},{4,20},{20... | collective-permute-start | bytes 1966088 | tf_op jit(solution)/shard_map/ppermute | solution.py:415

commit v8 on v7

--- a/solution.py
+++ b/solution.py
@@ -10,10 +10,10 @@
 DECAY = 1.0 - 2.0 ** (-0.8)
 MESH = pl.DeviceIdType.MESH
 LANES = 128
-CHUNK = 32
-FLIGHT = 4
+CHUNK = 64
+FLIGHT = 3
 PIECE = 128
-TAIL = 4
+TAIL = 2
 
 
 def adafactor(grad, weight, row_state, col_state, reduce_rows, reduce_cols, reduce_all, width, height):
@@ -300,11 +300,10 @@
         load.start()
     after = {
         per - 1: [moments_out],
-        per + 1: [columns_in],
-        per + 5: [moments_in, normalise],
-        per + 6: [tile_sums_in],
-        per + 7: [plane_sums_in],
-        per + 11: [scale_in, apply],
+        per: [columns_in],
+        per + 2: [moments_in, normalise],
+        per + 3: [tile_sums_in, plane_sums_in],
+        per + 4: [scale_in, apply],
     }
     for n in range(2 * total):
         e, k = divmod(n, per)

time: 237 us -> 237 us (level)
  no operation moved by 1% of the time
where the time goes in v8:
time: 237 us
  Pallas kernels  232 us (98%)
    pallas_call x1, Pallas kernels, fused_body(): pl.pallas_call(functools.partial(kernel, n_row, n_col), out_shape=(pltpu....  219 us
    pallas_call x1, Pallas kernels, written(): pl.pallas_call(writer, grid=(experts, rows // PIECE), out_shape=tuple((ja...  13.1 us
  transfers between devices with their start and end apart: 1, of which 1 were waited for; matrix products, arithmetic and copies ran while one was open for 0% of the time, Pallas kernels for 6%

profile of v8, /device:TPU:0, one launch (start us, length us, event | category | flops | bytes accessed | tf_op | source)
XLA Modules:
  0.0 236.6 jit_solution(10643414084507843237)
XLA Ops:
  0.6 219.2 %fused_step.1 = (f32[2,1024,1280]{2,1,0:T(8,128)}, f32[2,512]{1,0:T(2,128)S(1)}, f32[2,1280]{1,0:T(2,128)S(1)}, f32[128,1280]{1,0:T(8,128)}) custom-call(f32[1,2,1024,1280]{3,2,1,0:T(8,128)} %gp.1, f32[2,512,1280]{2,1,0:T(8,128)} %w.1, f32[2,512]{1,0:T(2,128)} %rs_in.1, f32[2,1280]{1,0:T(2,128)} %cs_in.1), custom_call_target="tpu_custom_call" | custom-call | flops 26214400 | bytes 26214400 | tf_op jit(solution)/shard_map/fused_step/pallas_call | solution.py:363
  219.8 0.6 collective-permute-start
  220.4 13.1 %write_out.1 = (f32[2,1024,1280]{2,1,0:T(8,128)}, f32[2,512]{1,0:T(2,128)}, f32[2,1280]{1,0:T(2,128)}) custom-call(f32[2,1024,1280]{2,1,0:T(8,128)} %get-tuple-element.10.a, f32[2,512]{1,0:T(2,128)S(1)} %get-tuple-element.11.b, f32[2,1280]{1,0:T(2,128)S(1)} %get-tuple-element.12.c), custom_call_target="tpu_custom_call" | custom-call | bytes 20971520 | tf_op jit(solution)/shard_map/write_out/pallas_call | solution.py:341
  233.5 2.2 collective-permute-done
  235.7 0.9 bitcast_dynamic-update-slice_fusion
Async XLA Ops:
  219.8 15.9 %collective-permute-start = (f32[128,1280]{1,0:T(8,128)}, f32[128,1280]{1,0:T(8,128)S(1)}, u32[]{:S(2)}, u32[]{:S(2)}) collective-permute-start(f32[128,1280]{1,0:T(8,128)} %get-tuple-element.14), channel_id=1, source_target_pairs={{0,16},{16,0},{1,17},{17,1},{2,18},{18,2},{3,19},{19,3},{4,20},{20... | collective-permute-start | bytes 1966088 | tf_op jit(solution)/shard_map/ppermute | solution.py:414
